TPU v7x, 768 devices: a whole 4x8x12 slice. The times are simulated.
768 devices in a mesh: row: 96 (over z, x, core), col: 8 (over y).
Axes of the slice: x: 4, y: 8, z: 12, core: 2. Of those that a mesh axis runs over, the one named last changes fastest.
Arguments:
- amplitudes: bfloat16 [96, 16, 393216], P(None, 'col', 'row'), may hold values from -20 to 20
- integrals: bfloat16 [3072, 8, 128, 128], P('row'), may hold values from -0.0390625 to 0.0390625
- tile_cols: int32 [3072, 8], P('row'), may hold values from -1 to 15, as said below
- pair_energy: float32 [96, 16], P('row'), may hold values from -2.5 to -1
- col_energy: float32 [2048], P('col'), may hold values from 0.2 to 1.5
Outputs:
- updated: bfloat16 [96, 16, 2048], P('row', None, 'col')
Inputs may be any that keep to these rules, and one draw needn't show every extreme that they name: `tile_cols`: in each row the live entries come first and name distinct column tiles; the remaining entries are -1. Every cd tile has at least one live entry, and among the 32 cd tiles of each index of row one has all 8 entries live.
All inputs are finite; a program needn't handle non-finite values.
Results may differ from a plain program's by a relative error of at most 0.0024.
Values sent between devices are 32-bit elements; how exact they have to be, the bound alone decides.
No kernel may reach another device: no remote copies, remote signals or barrier semaphores. Data moves between devices by JAX's collectives and lax.ppermute only.
A program may use at most 64 MiB of HBM per device.

v0:
```python
import jax
import jax.numpy as jnp
from jax import lax
from jax.sharding import PartitionSpec as P

NJ = 16


def partial_ladder(rows, integrals, tile_cols):
    blocks_here, pairs, _ = rows.shape
    tiles_here, slots, tile_len, _ = integrals.shape
    count = blocks_here * pairs
    groups = tiles_here // 8
    matches = tile_cols[:, :, None] == jnp.arange(NJ, dtype=jnp.int32)[None, None, :]
    left_all = rows.reshape(count, groups, 8 * tile_len).transpose(1, 0, 2)
    right_all = integrals.reshape(groups, 8, slots, tile_len, tile_len)
    pick_all = matches.reshape(groups, 8, slots, NJ)
    zero = jnp.zeros((), jnp.bfloat16)

    def step(acc, inputs):
        left, right, pick = inputs
        placed = jnp.where(pick[:, :, None, :, None], right[:, :, :, None, :], zero)
        dense = jnp.sum(placed, axis=1, dtype=jnp.bfloat16).reshape(8 * tile_len, NJ * tile_len)
        return (acc + jnp.dot(left, dense, preferred_element_type=jnp.float32), None)

    start = jnp.zeros((count, NJ * tile_len), jnp.float32)
    ladder, _ = lax.scan(step, start, (left_all, right_all, pick_all))
    return ladder.reshape(blocks_here, pairs, NJ * tile_len)


def per_device(amplitudes, integrals, tile_cols, pair_energy, col_energy):
    whole = partial_ladder(amplitudes, integrals, tile_cols)
    moved = lax.all_to_all(whole, "col", split_axis=2, concat_axis=1, tiled=True)
    owned = lax.psum_scatter(moved, "row", scatter_dimension=0, tiled=True)
    denom = pair_energy[:, :, None] - col_energy[None, None, :]
    return (owned / denom).astype(jnp.bfloat16)


def solution(mesh):
    in_specs = (
        P(None, "col", "row"),
        P("row", None, None, None),
        P("row", None),
        P("row", None),
        P("col"),
    )
    out_specs = P("row", None, "col")
    return jax.shard_map(
        per_device, mesh=mesh, in_specs=in_specs, out_specs=out_specs, check_vma=False
    )
```

profile of v0, /device:TPU:8, one launch (start us, length us, event | category | flops | bytes accessed | tf_op | source)
XLA Modules:
  0.0 386.8 jit_solution(4875781190404820133)
XLA Ops:
  6.5 0.0 reduce-scatter.2.cloned.1.call-start
  6.5 2.8 reshape.75
  9.3 0.0 copy-start
  9.3 1.6 copy.22
  11.0 0.0 copy-done
  11.0 0.1 copy.25
  11.1 0.1 iota_compare_fusion
  11.2 83.5 %while.11 = (s32[]{:T(128)}, f32[192,2048]{1,0:T(8,128)}, bf16[4,192,1024]{2,1,0:T(8,128)(2,1)}, pred[4,8,8,16]{3,2,1,0:T(8,128)(4,1)S(1)}, bf16[4,8,8,128,128]{4,3,2,1,0:T(8,128)(2,1)}, /*index=5*/s32[]{:T(128)}, s32[]{:T(128)}) while((s32[]{:T(128)}, f32[192,2048]{1,0:T(8,128)}, bf16[4,192,1024]{2,1,0:T(8,128)(2,1)}, ...), condition=%wide.region_2.3_spmd.clone, body=%wide.region_0.2_spmd.clone.sunk | while | flops 837550080 | bytes 18222688 | solution.py:27
  11.2 1.7 dynamic-slice_bitcast_fusion.5
  12.9 14.2 %select_reduce_fusion.2 = bf16[8,128,16,128]{3,2,1,0:T(8,128)(2,1)} fusion(pred[8,8,16]{2,1,0:T(8,128)(4,1)S(1)} %dynamic-slice_bitcast_fusion.4, bf16[8,8,128,128]{3,2,1,0:T(8,128)(2,1)S(1)} %dynamic-slice_bitcast_fusion.5), kind=kLoop, calls=%fused_computation.clone.1 | loop fusion | flops 31457280 | bytes 6292480 | tf_op jit(solution)/shard_map/while/body/eval_jaxpr/reduce_sum | solution.py:23
  27.1 4.5 %fusion.14 = f32[192,2048]{1,0:T(8,128)} fusion(bf16[128,8,16,128]{3,2,1,0:T(8,128)(2,1)} %bitcast.31, f32[192,2048]{1,0:T(8,128)} %get-tuple-element.125, pred[]{:T(512)S(6)} %compare.3, bf16[4,192,1024]{2,1,0:T(8,128)(2,1)} %get-tuple-element.133, s32[]{:T(128)} %get-tuple-element.124), kind=kOutput, calls=%fused_computation.4.clone.1 | convolution fusion | flops 806092800 | bytes 7733761 | tf_op jit(solution)/shard_map/while/body/eval_jaxpr/dot_general | solution.py:24
  31.7 1.7 dynamic-slice_bitcast_fusion.5
  33.4 14.2 %select_reduce_fusion.2 = bf16[8,128,16,128]{3,2,1,0:T(8,128)(2,1)} fusion(pred[8,8,16]{2,1,0:T(8,128)(4,1)S(1)} %dynamic-slice_bitcast_fusion.4, bf16[8,8,128,128]{3,2,1,0:T(8,128)(2,1)S(1)} %dynamic-slice_bitcast_fusion.5), kind=kLoop, calls=%fused_computation.clone.1 | loop fusion | flops 31457280 | bytes 6292480 | tf_op jit(solution)/shard_map/while/body/eval_jaxpr/reduce_sum | solution.py:23
  47.6 5.0 %fusion.14 = f32[192,2048]{1,0:T(8,128)} fusion(bf16[128,8,16,128]{3,2,1,0:T(8,128)(2,1)} %bitcast.31, f32[192,2048]{1,0:T(8,128)} %get-tuple-element.125, pred[]{:T(512)S(6)} %compare.3, bf16[4,192,1024]{2,1,0:T(8,128)(2,1)} %get-tuple-element.133, s32[]{:T(128)} %get-tuple-element.124), kind=kOutput, calls=%fused_computation.4.clone.1 | convolution fusion | flops 806092800 | bytes 7733761 | tf_op jit(solution)/shard_map/while/body/eval_jaxpr/dot_general | solution.py:24
  52.7 1.7 dynamic-slice_bitcast_fusion.5
  54.4 14.2 %select_reduce_fusion.2 = bf16[8,128,16,128]{3,2,1,0:T(8,128)(2,1)} fusion(pred[8,8,16]{2,1,0:T(8,128)(4,1)S(1)} %dynamic-slice_bitcast_fusion.4, bf16[8,8,128,128]{3,2,1,0:T(8,128)(2,1)S(1)} %dynamic-slice_bitcast_fusion.5), kind=kLoop, calls=%fused_computation.clone.1 | loop fusion | flops 31457280 | bytes 6292480 | tf_op jit(solution)/shard_map/while/body/eval_jaxpr/reduce_sum | solution.py:23
  68.6 5.0 %fusion.14 = f32[192,2048]{1,0:T(8,128)} fusion(bf16[128,8,16,128]{3,2,1,0:T(8,128)(2,1)} %bitcast.31, f32[192,2048]{1,0:T(8,128)} %get-tuple-element.125, pred[]{:T(512)S(6)} %compare.3, bf16[4,192,1024]{2,1,0:T(8,128)(2,1)} %get-tuple-element.133, s32[]{:T(128)} %get-tuple-element.124), kind=kOutput, calls=%fused_computation.4.clone.1 | convolution fusion | flops 806092800 | bytes 7733761 | tf_op jit(solution)/shard_map/while/body/eval_jaxpr/dot_general | solution.py:24
  73.6 1.7 dynamic-slice_bitcast_fusion.5
  75.4 14.2 %select_reduce_fusion.2 = bf16[8,128,16,128]{3,2,1,0:T(8,128)(2,1)} fusion(pred[8,8,16]{2,1,0:T(8,128)(4,1)S(1)} %dynamic-slice_bitcast_fusion.4, bf16[8,8,128,128]{3,2,1,0:T(8,128)(2,1)S(1)} %dynamic-slice_bitcast_fusion.5), kind=kLoop, calls=%fused_computation.clone.1 | loop fusion | flops 31457280 | bytes 6292480 | tf_op jit(solution)/shard_map/while/body/eval_jaxpr/reduce_sum | solution.py:23
  89.6 5.0 %fusion.14 = f32[192,2048]{1,0:T(8,128)} fusion(bf16[128,8,16,128]{3,2,1,0:T(8,128)(2,1)} %bitcast.31, f32[192,2048]{1,0:T(8,128)} %get-tuple-element.125, pred[]{:T(512)S(6)} %compare.3, bf16[4,192,1024]{2,1,0:T(8,128)(2,1)} %get-tuple-element.133, s32[]{:T(128)} %get-tuple-element.124), kind=kOutput, calls=%fused_computation.4.clone.1 | convolution fusion | flops 806092800 | bytes 7733761 | tf_op jit(solution)/shard_map/while/body/eval_jaxpr/dot_general | solution.py:24
  94.6 3.0 reshape.77
  97.6 4.2 %copy.23 = f32[96,2,2048]{0,1,2:T(2,128)S(1)} copy(f32[96,2,2048]{2,1,0:T(2,128)} %reshape.77) | data formatting | bytes 3145728 | tf_op jit(solution)/shard_map/reshape | solution.py:28
  101.8 57.2 %all_to_all.18 = f32[96,2,2048]{0,1,2:T(2,128)} all-to-all(f32[96,2,2048]{0,1,2:T(2,128)S(1)} %copy.23), channel_id=1, replica_groups=mesh['row'=96,'col'=8] {'col'}, dimensions={2} | all-to-all | bytes 3145728 | tf_op jit(solution)/shard_map/all_to_all | solution.py:33
  159.0 4.3 %copy.24 = f32[96,8,2,256]{3,2,1,0:T(2,128)S(1)} copy(f32[96,8,2,256]{0,2,3,1:T(2,128)} %bitcast.33) | data formatting | bytes 3145728 | tf_op jit(solution)/shard_map/all_to_all | solution.py:33
  163.3 2.2 all_to_all.16
  165.6 0.0 copy-start.1
  165.6 0.0 copy-start.2
  165.6 0.0 reduce-scatter.2.cloned.1.call-update
  165.6 212.9 %reduce-scatter.2.cloned.1.call-done = f32[1,16,256]{2,1,0:T(8,128)} async-done(((f32[96,16,256]{2,1,0:T(8,128)}), f32[1,16,256]{2,1,0:T(8,128)}) %reduce-scatter.2.cloned.1.call-update) | async-done | bytes 16400 | tf_op jit(solution)/shard_map/reduce_scatter | solution.py:34
  378.5 0.0 copy-done.1
  378.5 0.0 copy-done.2
  378.6 1.4 divide_convert_fusion
  (5 shorter events, 0.0 us)
Async XLA Ops:
  6.5 372.0 %reduce-scatter.2.cloned.1.call-start = ((), (), s32[]{:S(2)}) async-start(), calls=%async_computation.2 | async-start | bytes 1589248 | tf_op jit(solution)/shard_map/reduce_scatter | solution.py:34
  9.3 1.7 copy-start
  165.6 213.0 %copy-start.1 = (f32[256]{0:T(256)S(1)}, f32[256]{0:T(256)}, u32[]{:S(2)}) copy-start(f32[256]{0:T(256)} %param.11) | copy-start | bytes 3076
  165.6 213.0 %copy-start.2 = (f32[1,16]{1,0:T(1,128)S(1)}, f32[1,16]{1,0:T(1,128)}, u32[]{:S(2)}) copy-start(f32[1,16]{1,0:T(1,128)} %param.10) | copy-start | bytes 196
Sparse Core Ops, SparseCore 0:
  165.7 212.7 reduce-scatter.1
where the time goes:
time: 387 us
  waiting for transfers between devices  213 us (55%)
  other arithmetic  58.3 us (15%)
  blocking collectives  57.2 us (15%)
  local copies, waits for them, and re-layouts  25.2 us (7%)
  matrix products  19.6 us (5%)
  between operations  13.4 us (3%)
    reduce_scatter x1, waiting for transfers between devices, per_device(): owned = lax.psum_scatter(moved, 'row', scatter_dimension=0, tiled=True)  213 us
    all_to_all x1, blocking collectives, per_device(): lax.all_to_all(whole, 'col', split_axis=2, concat_axis=1, tiled=True)  57.2 us
    reduce_sum x4, other arithmetic, step(): jnp.sum(placed, axis=1, dtype=jnp.bfloat16)  56.8 us
    dot_general x4, matrix products, step(): jnp.dot(left, dense, preferred_element_type=jnp.float32)  19.6 us
  transfers between devices with their start and end apart: 1, of which 1 were waited for; matrix products, arithmetic and copies ran while one was open for 0% of the time, Pallas kernels for 0%

commit v1 on v0

v1 whole, which is shorter than its diff:
```python
import jax
import jax.numpy as jnp
from jax import lax
from jax.experimental import pallas as pl
from jax.experimental.pallas import tpu as pltpu
from jax.sharding import Mesh, PartitionSpec as P

NJ = 16
TILE = 128
NZ, NX, NC, NY = 12, 4, 2, 8
ROW = ("z", "x", "core")
CHUNKS = 4


def ladder_kernel(cols_ref, left_ref, tiles_hbm, out_ref, tiles_ref, where_ref, sems):
    kr, slots = cols_ref.shape
    per = kr // CHUNKS
    empty = kr * slots

    def chunk(c):
        span = pl.ds(c * per * slots, per * slots)
        return pltpu.make_async_copy(tiles_hbm.at[span], tiles_ref.at[span], sems.at[c])

    for c in range(CHUNKS):
        chunk(c).start()
    tiles_ref[empty] = jnp.zeros((TILE, TILE), jnp.bfloat16)

    def locate(k, carry):
        for j in range(NJ + 1):
            where_ref[k * (NJ + 1) + j] = empty
        for s in range(slots):
            where_ref[k * (NJ + 1) + cols_ref[k, s] + 1] = k * slots + s
        return carry

    lax.fori_loop(0, kr, locate, 0)

    def tile(k, j):
        return tiles_ref[where_ref[k * (NJ + 1) + j + 1]]

    def pair(k, j):
        return jnp.concatenate([tile(k, j), tile(k + 1, j)], axis=0)

    for c in range(CHUNKS):
        chunk(c).wait()
        for j in range(0, NJ, 2):
            span = pl.ds(j * TILE, 2 * TILE)
            acc = None if c == 0 else out_ref[:, span]
            for k in range(c * per, (c + 1) * per, 2):
                right = jnp.concatenate([pair(k, j), pair(k, j + 1)], axis=1)
                part = jnp.dot(
                    left_ref[:, pl.ds(k * TILE, 2 * TILE)], right,
                    preferred_element_type=jnp.float32,
                )
                acc = part if acc is None else acc + part
            out_ref[:, span] = acc


def ladder(left, integrals, tile_cols):
    kr, slots, _, _ = integrals.shape
    rows = left.shape[0]
    return pl.pallas_call(
        ladder_kernel,
        out_shape=jax.ShapeDtypeStruct((rows, NJ * TILE), jnp.float32),
        in_specs=[
            pl.BlockSpec(memory_space=pltpu.SMEM),
            pl.BlockSpec(memory_space=pltpu.VMEM),
            pl.BlockSpec(memory_space=pl.ANY),
        ],
        out_specs=pl.BlockSpec(memory_space=pltpu.VMEM),
        scratch_shapes=[
            pltpu.VMEM((kr * slots + 1, TILE, TILE), jnp.bfloat16),
            pltpu.SMEM((kr * (NJ + 1),), jnp.int32),
            pltpu.SemaphoreType.DMA((CHUNKS,)),
        ],
        compiler_params=pltpu.CompilerParams(vmem_limit_bytes=40 * 2**20),
    )(tile_cols, left, integrals.reshape(kr * slots, TILE, TILE))


def per_device(amplitudes, integrals, tile_cols, pair_energy, col_energy):
    blocks, pairs, depth = amplitudes.shape
    left = amplitudes.reshape(NZ, NX, NC, pairs, depth).transpose(2, 1, 0, 3, 4)
    left = left.reshape(blocks * pairs, depth)
    whole = ladder(left, integrals, tile_cols)
    half = blocks * pairs // NC
    core = lax.axis_index("core")
    mine = lax.dynamic_slice_in_dim(whole, core * half, half, 0)
    other = lax.dynamic_slice_in_dim(whole, (1 - core) * half, half, 0)
    other = lax.ppermute(other, "core", [(0, 1), (1, 0)])
    chip = (mine + other).reshape(NX, NZ * pairs, NJ * TILE)
    chip = lax.all_to_all(chip, "x", 0, 0, tiled=True)
    plane = jnp.sum(chip, axis=0)
    plane = plane.reshape(NZ, pairs, NY, NJ * TILE // NY).transpose(0, 2, 1, 3)
    plane = plane.reshape(NZ * NY, pairs, NJ * TILE // NY)
    owned = lax.all_to_all(plane, ("z", "y"), 0, 0, tiled=True)
    owned = jnp.sum(owned.reshape(NZ, NY * pairs, NJ * TILE // NY), axis=0, keepdims=True)
    denom = pair_energy[:, :, None] - col_energy[None, None, :]
    return (owned / denom).astype(jnp.bfloat16)


def solution(mesh):
    fine = Mesh(mesh.devices.reshape(NZ, NX, NC, NY), ("z", "x", "core", "y"))
    in_specs = (
        P(None, "y", ROW),
        P(ROW, None, None, None),
        P(ROW, None),
        P(ROW, None),
        P("y"),
    )
    out_specs = P(ROW, None, "y")
    return jax.shard_map(
        per_device, mesh=fine, in_specs=in_specs, out_specs=out_specs, check_vma=False
    )
```

time: 387 us -> 74.3 us (0.19)
  waiting for transfers between devices: 213 us -> 2.25 us
  other arithmetic: 58.3 us -> 0.83 us
  matrix products: 19.6 us -> 0 us
  local copies, waits for them, and re-layouts: 25.2 us -> 8.56 us
  between operations: 13.4 us -> 0.12 us
  Pallas kernels: 0 us -> 5.88 us
    reduce_scatter x1 -> x0, waiting for transfers between devices: 213 us -> none  [per_device(): owned = lax.psum_scatter(moved, 'row', scatter_dimension=0, tiled=True)]
    reduce_sum x4 -> x2, other arithmetic: 56.8 us -> 0.06 us  [the longest x1 0.04 us: per_device(): plane = jnp.sum(chip, axis=0)]
    dot_general x4 -> x0, matrix products: 19.6 us -> none  [step(): jnp.dot(left, dense, preferred_element_type=jnp.float32)]
    broadcast_in_dim x8 -> x0, local copies, waits for them, and re-layouts: 6.95 us -> none  [step(): placed = jnp.where(pick[:, :, None, :, None], right[:, :, :, None, :], zero)]
    all_to_all x2 -> x0, local copies, waits for them, and re-layouts: 6.54 us -> none  [per_device(): lax.all_to_all(whole, 'col', split_axis=2, concat_axis=1, tiled=True)]
    pallas_call x0 -> x1, Pallas kernels: none -> 5.88 us  [ladder(): pl.pallas_call(ladder_kernel, out_shape=jax.ShapeDtypeStruct((rows, NJ *...]
    reshape x3 -> x4, local copies, waits for them, and re-layouts: 9.98 us -> 4.27 us  [the longest x1 3.33 us: per_device(): left = amplitudes.reshape(NZ, NX, NC, pairs, depth).transpose(2, 1, 0, 3, 4)]
    all_to_all x1 -> x2, blocking collectives: 57.2 us -> 54.4 us  [the longest x1 37.7 us: per_device(): owned = lax.all_to_all(plane, ('z', 'y'), 0, 0, tiled=True)]
where the time goes in v1:
time: 74.3 us; the launch traced here: 74 us
  blocking collectives  54.4 us (73%)
  local copies, waits for them, and re-layouts  8.56 us (12%)
  Pallas kernels  5.88 us (8%)
  waiting for transfers between devices  2.25 us (3%)
  starting transfers between devices  1.92 us (3%)
  other arithmetic  0.83 us (1%)
    all_to_all x1, blocking collectives, per_device(): owned = lax.all_to_all(plane, ('z', 'y'), 0, 0, tiled=True)  37.7 us
    all_to_all x1, blocking collectives, per_device(): chip = lax.all_to_all(chip, 'x', 0, 0, tiled=True)  16.7 us
    pallas_call x1, Pallas kernels, ladder(): pl.pallas_call(ladder_kernel, out_shape=jax.ShapeDtypeStruct((rows, NJ *...  5.88 us
    unnamed x8, local copies, waits for them, and re-layouts  4.21 us
    reshape x1, local copies, waits for them, and re-layouts, per_device(): left = amplitudes.reshape(NZ, NX, NC, pairs, depth).transpose(2, 1, 0, 3, 4)  3.33 us
    ppermute x1, waiting for transfers between devices, per_device(): other = lax.ppermute(other, 'core', [(0, 1), (1, 0)])  2.25 us
    ppermute x1, starting transfers between devices, per_device(): other = lax.ppermute(other, 'core', [(0, 1), (1, 0)])  1.92 us
  transfers between devices with their start and end apart: 1, of which 1 were waited for; matrix products, arithmetic and copies ran while one was open for 0% of the time, Pallas kernels for 0%

profile of v1, /device:TPU:8, one launch (start us, length us, event | category | flops | bytes accessed | tf_op | source)
XLA Modules:
  0.0 74.0 jit_solution(15588137028905191025)
XLA Ops:
  0.0 0.8 %copy.15.cols_ref = s32[32,8]{1,0:T(8,128)S(1)} copy(s32[32,8]{0,1:T(8,128)} %param.7) | data formatting | bytes 2048 | tf_op args[2]
  0.8 3.3 %copy.21 = bf16[12,4,2,2,4096]{4,3,0,1,2:T(2,128)(2,1)S(1)} copy(bf16[12,4,2,2,4096]{4,3,2,1,0:T(2,128)(2,1)} %bitcast.22) | data formatting | bytes 3145728 | tf_op jit(solution)/shard_map/reshape | solution.py:81
  4.1 0.6 reshape.89.left_ref
  4.8 0.0 copy-start
  4.8 3.4 %copy-done = bf16[32,8,128,128]{3,2,1,0:T(8,128)(2,1)S(1)} copy-done((bf16[32,8,128,128]{3,2,1,0:T(8,128)(2,1)S(1)}, bf16[32,8,128,128]{3,2,1,0:T(8,128)(2,1)}, u32[]{:S(2)}) %copy-start) | copy-done | bytes 8388632
  8.1 5.9 %shard_map.58 = f32[192,2048]{1,0:T(8,128)S(1)} custom-call(s32[32,8]{1,0:T(8,128)S(1)} %copy.15.cols_ref, bf16[192,4096]{1,0:T(8,128)(2,1)S(1)} %reshape.89.left_ref, bf16[256,128,128]{2,1,0:T(8,128)(2,1)S(1)} %bitcast.19), custom_call_target="tpu_custom_call" | custom-call | tf_op jit(solution)/shard_map/pallas_call | solution.py:61
  14.0 0.1 constant_dynamic-slice_fusion
  14.1 1.9 %collective-permute-start = (f32[96,2048]{1,0:T(8,128)S(1)}, f32[96,2048]{1,0:T(8,128)S(1)}, u32[]{:S(2)}, u32[]{:S(2)}) collective-permute-start(f32[96,2048]{1,0:T(8,128)S(1)} %constant_dynamic-slice_fusion), channel_id=1, source_target_pairs={{0,8},{8,0},{1,9},{9,1},{2,10},{10,2},{3,11},{11,3},{4,12},{12,4},... | collective-permute-start | bytes 2359304 | tf_op jit(solution)/shard_map/ppermute | solution.py:88
  16.0 2.2 %collective-permute-done = f32[96,2048]{1,0:T(8,128)S(1)} collective-permute-done((f32[96,2048]{1,0:T(8,128)S(1)}, f32[96,2048]{1,0:T(8,128)S(1)}, u32[]{:S(2)}, u32[]{:S(2)}) %collective-permute-start) | collective-permute-done | bytes 786464 | tf_op jit(solution)/shard_map/ppermute | solution.py:88
  18.3 0.1 dynamic-slice_add_fusion
  18.4 16.7 %all_to_all.10 = f32[4,24,2048]{2,1,0:T(8,128)S(1)} all-to-all(f32[4,24,2048]{2,1,0:T(8,128)S(1)} %bitcast.21), channel_id=1, replica_groups=mesh['z'=12,'x'=4,'core'=2,'y'=8] {'x'}, dimensions={0} | all-to-all | bytes 1572864 | tf_op jit(solution)/shard_map/all_to_all | solution.py:90
  35.1 0.0 copy-start.1
  35.1 0.0 copy-start.2
  35.1 0.1 copy.18
  35.2 0.2 copy.17
  35.4 37.7 %all_to_all.11 = f32[96,2,256]{2,1,0:T(2,128)S(1)} all-to-all(f32[96,2,256]{2,1,0:T(2,128)S(1)} %copy.17), channel_id=1, replica_groups=mesh['z'=12,'x'=4,'core'=2,'y'=8] {'z','y'}, dimensions={0} | all-to-all | bytes 393216 | tf_op jit(solution)/shard_map/all_to_all | solution.py:94
  73.1 0.1 reshape.94
  73.3 0.0 copy-done.1
  73.3 0.0 copy-done.2
  73.3 0.7 fusion
  (3 shorter events, 0.1 us)
Async XLA Ops:
  4.8 3.4 %copy-start = (bf16[32,8,128,128]{3,2,1,0:T(8,128)(2,1)S(1)}, bf16[32,8,128,128]{3,2,1,0:T(8,128)(2,1)}, u32[]{:S(2)}) copy-start(bf16[32,8,128,128]{3,2,1,0:T(8,128)(2,1)} %param.6) | copy-start | bytes 25165828
  14.1 4.2 %collective-permute-start = (f32[96,2048]{1,0:T(8,128)S(1)}, f32[96,2048]{1,0:T(8,128)S(1)}, u32[]{:S(2)}, u32[]{:S(2)}) collective-permute-start(f32[96,2048]{1,0:T(8,128)S(1)} %constant_dynamic-slice_fusion), channel_id=1, source_target_pairs={{0,8},{8,0},{1,9},{9,1},{2,10},{10,2},{3,11},{11,3},{4,12},{12,4},... | collective-permute-start | bytes 2359304 | tf_op jit(solution)/shard_map/ppermute | solution.py:88
  35.1 38.2 %copy-start.1 = (f32[256]{0:T(256)S(1)}, f32[256]{0:T(256)}, u32[]{:S(2)}) copy-start(f32[256]{0:T(256)} %param.9) | copy-start | bytes 3076
  35.1 38.2 %copy-start.2 = (f32[1,16]{1,0:T(1,128)S(1)}, f32[1,16]{1,0:T(1,128)}, u32[]{:S(2)}) copy-start(f32[1,16]{1,0:T(1,128)} %param.8) | copy-start | bytes 196

commit v2 on v1

v2 whole, which is shorter than its diff:
```python
import jax
import jax.numpy as jnp
from jax import lax
from jax.experimental import pallas as pl
from jax.experimental.pallas import tpu as pltpu
from jax.sharding import Mesh, PartitionSpec as P

NJ = 16
TILE = 128
NZ, NX, NC, NY = 12, 4, 2, 8
ROW = ("z", "x", "core")
CHUNKS = 4
AHEAD = 2
LIMIT = 52 * 2**20


def ladder_kernel(core_ref, cols_hbm, left_hbm, tiles_hbm, send_ref, keep_ref,
                  cols_ref, left_ref, tiles_ref, where_ref, cols_sem, left_sems, tile_sems):
    slots, kr = cols_ref.shape
    half, width = send_ref.shape
    per = kr // CHUNKS
    empty = kr * slots
    stride = NJ + 1
    core = core_ref[0]

    def copies(c):
        depth = pl.ds(c * per * TILE, per * TILE)
        span = pl.ds(c * per * slots, per * slots)
        return (
            pltpu.make_async_copy(left_hbm.at[..., depth], left_ref.at[..., depth], left_sems.at[c]),
            pltpu.make_async_copy(tiles_hbm.at[span], tiles_ref.at[span], tile_sems.at[c]),
        )

    def start(c):
        for copy in copies(c):
            copy.start()

    fetch = pltpu.make_async_copy(cols_hbm, cols_ref, cols_sem)
    fetch.start()
    for c in range(AHEAD):
        start(c)
    tiles_ref[empty] = jnp.zeros((TILE, TILE), jnp.bfloat16)
    for at in range(kr * stride):
        where_ref[at] = empty
    fetch.wait()
    for k in range(kr):
        found = [cols_ref[s, k] for s in range(slots)]
        for s in range(slots):
            where_ref[k * stride + found[s] + 1] = k * slots + s

    def column(first, j):
        return jnp.concatenate(
            [tiles_ref[where_ref[(first + i) * stride + j + 1]] for i in range(per)], axis=0
        )

    for c in range(CHUNKS):
        for copy in copies(c):
            copy.wait()
        if c + AHEAD < CHUNKS:
            start(c + AHEAD)
        first = c * per
        depth = pl.ds(first * TILE, per * TILE)
        left = jnp.concatenate(
            [left_ref[:, x, side, :, depth] for side in (1 - core, core) for x in range(NX)],
            axis=0,
        ).reshape(2 * half, per * TILE)
        for j in range(0, NJ, 2):
            span = pl.ds(j * TILE, 2 * TILE)
            right = jnp.concatenate([column(first, j), column(first, j + 1)], axis=1)
            part = jnp.dot(left, right, preferred_element_type=jnp.float32)
            if c == 0:
                send_ref[:, span] = part[:half]
                keep_ref[:, span] = part[half:]
            else:
                send_ref[:, span] += part[:half]
                keep_ref[:, span] += part[half:]


def ladder(core, left, integrals, tile_cols):
    kr, slots, _, _ = integrals.shape
    blocks, pairs, depth = left.shape
    left = left.reshape(NZ, NX, NC, pairs, depth)
    half = jax.ShapeDtypeStruct((blocks * pairs // NC, NJ * TILE), jnp.float32)
    return pl.pallas_call(
        ladder_kernel,
        out_shape=(half, half),
        in_specs=[
            pl.BlockSpec(memory_space=pltpu.SMEM),
            pl.BlockSpec(memory_space=pl.ANY),
            pl.BlockSpec(memory_space=pl.ANY),
            pl.BlockSpec(memory_space=pl.ANY),
        ],
        out_specs=(pl.BlockSpec(memory_space=pltpu.VMEM), pl.BlockSpec(memory_space=pltpu.VMEM)),
        scratch_shapes=[
            pltpu.SMEM((slots, kr), jnp.int32),
            pltpu.VMEM(left.shape, jnp.bfloat16),
            pltpu.VMEM((kr * slots + 1, TILE, TILE), jnp.bfloat16),
            pltpu.SMEM((kr * (NJ + 1),), jnp.int32),
            pltpu.SemaphoreType.DMA(()),
            pltpu.SemaphoreType.DMA((CHUNKS,)),
            pltpu.SemaphoreType.DMA((CHUNKS,)),
        ],
        compiler_params=pltpu.CompilerParams(vmem_limit_bytes=LIMIT),
    )(core.reshape(1), tile_cols.T, left, integrals.reshape(kr * slots, TILE, TILE))


def per_device(amplitudes, integrals, tile_cols, pair_energy, col_energy):
    pairs = amplitudes.shape[1]
    core = lax.axis_index("core")
    send, keep = ladder(core, amplitudes, integrals, tile_cols)
    other = lax.ppermute(send, "core", [(0, 1), (1, 0)])
    chip = (keep + other).reshape(NX, NZ * pairs, NJ * TILE)
    chip = lax.all_to_all(chip, "x", 0, 0, tiled=True)
    plane = jnp.sum(chip, axis=0)
    plane = plane.reshape(NZ, pairs, NY, NJ * TILE // NY).transpose(0, 2, 1, 3)
    plane = plane.reshape(NZ * NY, pairs, NJ * TILE // NY)
    owned = lax.all_to_all(plane, ("z", "y"), 0, 0, tiled=True)
    owned = jnp.sum(owned.reshape(NZ, NY * pairs, NJ * TILE // NY), axis=0, keepdims=True)
    denom = pair_energy[:, :, None] - col_energy[None, None, :]
    return (owned / denom).astype(jnp.bfloat16)


def solution(mesh):
    fine = Mesh(mesh.devices.reshape(NZ, NX, NC, NY), ("z", "x", "core", "y"))
    in_specs = (
        P(None, "y", ROW),
        P(ROW, None, None, None),
        P(ROW, None),
        P(ROW, None),
        P("y"),
    )
    out_specs = P(ROW, None, "y")
    return jax.shard_map(
        per_device, mesh=fine, in_specs=in_specs, out_specs=out_specs, check_vma=False
    )
```

time: 74.3 us -> 66.2 us (0.89)
  local copies, waits for them, and re-layouts: 8.56 us -> 1.06 us
    reshape x2 -> x0, local copies, waits for them, and re-layouts: 3.98 us -> none  [the longest x1 3.33 us: per_device(): left = amplitudes.reshape(NZ, NX, NC, pairs, depth).transpose(2, 1, 0, 3, 4)]
    unnamed x8 -> x7, local copies, waits for them, and re-layouts: 4.21 us -> 0.76 us
where the time goes in v2:
time: 66.2 us; the launch traced here: 66 us
  blocking collectives  54.4 us (82%)
  Pallas kernels  5.41 us (8%)
  waiting for transfers between devices  2.25 us (3%)
  starting transfers between devices  1.92 us (3%)
  local copies, waits for them, and re-layouts  1.06 us (2%)
  other arithmetic  0.85 us (1%)
    all_to_all x1, blocking collectives, per_device(): owned = lax.all_to_all(plane, ('z', 'y'), 0, 0, tiled=True)  37.7 us
    all_to_all x1, blocking collectives, per_device(): chip = lax.all_to_all(chip, 'x', 0, 0, tiled=True)  16.7 us
    pallas_call x1, Pallas kernels, ladder(): pl.pallas_call(ladder_kernel, out_shape=(half, half), in_specs=[pl.BlockS...  5.41 us
    ppermute x1, waiting for transfers between devices, per_device(): other = lax.ppermute(send, 'core', [(0, 1), (1, 0)])  2.25 us
    ppermute x1, starting transfers between devices, per_device(): other = lax.ppermute(send, 'core', [(0, 1), (1, 0)])  1.92 us
  transfers between devices with their start and end apart: 1, of which 1 were waited for; matrix products, arithmetic and copies ran while one was open for 0% of the time, Pallas kernels for 0%

profile of v2, /device:TPU:8, one launch (start us, length us, event | category | flops | bytes accessed | tf_op | source)
XLA Modules:
  0.0 66.0 jit_solution(10092725066689003919)
XLA Ops:
  0.0 0.0 copy-start
  0.0 0.7 %copy-done = s32[32,8]{0,1:T(8,128)S(1)} copy-done((s32[32,8]{0,1:T(8,128)S(1)}, s32[32,8]{0,1:T(8,128)}, u32[]{:S(2)}) %copy-start) | copy-done | bytes 1048
  0.7 0.0 copy-start.1
  0.7 0.0 copy-start.2
  0.7 5.4 %shard_map.58 = (f32[96,2048]{1,0:T(8,128)S(1)}, f32[96,2048]{1,0:T(8,128)S(1)}) custom-call(s32[1]{0:T(128)} %bitcast.core_ref, s32[8,32]{1,0:T(8,128)S(1)} %bitcast.18, bf16[12,4,2,2,4096]{4,3,2,1,0:T(2,128)(2,1)} %bitcast.21, bf16[256,128,128]{2,1,0:T(8,128)(2,1)} %bitcast.19), custom_call_target="tpu_custom_call" | custom-call | tf_op jit(solution)/shard_map/pallas_call | solution.py:84
  6.1 1.9 %collective-permute-start = (f32[96,2048]{1,0:T(8,128)S(1)}, f32[96,2048]{1,0:T(8,128)S(1)}, u32[]{:S(2)}, u32[]{:S(2)}) collective-permute-start(f32[96,2048]{1,0:T(8,128)S(1)} %get-tuple-element.8), channel_id=1, source_target_pairs={{0,8},{8,0},{1,9},{9,1},{2,10},{10,2},{3,11},{11,3},{4,12},{12,4},... | collective-permute-start | bytes 2359304 | tf_op jit(solution)/shard_map/ppermute | solution.py:111
  8.0 2.3 %collective-permute-done = f32[96,2048]{1,0:T(8,128)S(1)} collective-permute-done((f32[96,2048]{1,0:T(8,128)S(1)}, f32[96,2048]{1,0:T(8,128)S(1)}, u32[]{:S(2)}, u32[]{:S(2)}) %collective-permute-start) | collective-permute-done | bytes 786464 | tf_op jit(solution)/shard_map/ppermute | solution.py:111
  10.3 0.1 add.3
  10.4 16.7 %all_to_all.10 = f32[4,24,2048]{2,1,0:T(8,128)S(1)} all-to-all(f32[4,24,2048]{2,1,0:T(8,128)S(1)} %bitcast.20), channel_id=1, replica_groups=mesh['z'=12,'x'=4,'core'=2,'y'=8] {'x'}, dimensions={0} | all-to-all | bytes 1572864 | tf_op jit(solution)/shard_map/all_to_all | solution.py:113
  27.1 0.1 copy.10
  27.2 0.2 copy.9
  27.4 37.7 %all_to_all.11 = f32[96,2,256]{2,1,0:T(2,128)S(1)} all-to-all(f32[96,2,256]{2,1,0:T(2,128)S(1)} %copy.9), channel_id=1, replica_groups=mesh['z'=12,'x'=4,'core'=2,'y'=8] {'z','y'}, dimensions={0} | all-to-all | bytes 393216 | tf_op jit(solution)/shard_map/all_to_all | solution.py:117
  65.1 0.1 reshape.94
  65.3 0.0 copy-done.1
  65.3 0.0 copy-done.2
  65.3 0.7 %fusion = bf16[1,16,256]{2,1,0:T(8,128)(2,1)} fusion(f32[16,256]{1,0:T(8,128)S(1)} %reduce_sum.21, f32[256]{0:T(256)S(1)} %copy-done.1, f32[16]{0:T(128)S(1)} %bitcast.25), kind=kLoop, calls=%fused_computation.2 | loop fusion | flops 12288 | bytes 25664 | tf_op jit(solution)/shard_map/convert_element_type | solution.py:120
  (3 shorter events, 0.1 us)
Async XLA Ops:
  0.0 0.7 %copy-start = (s32[32,8]{0,1:T(8,128)S(1)}, s32[32,8]{0,1:T(8,128)}, u32[]{:S(2)}) copy-start(s32[32,8]{0,1:T(8,128)} %param.7) | copy-start | bytes 3076
  0.7 64.6 %copy-start.1 = (f32[256]{0:T(256)S(1)}, f32[256]{0:T(256)}, u32[]{:S(2)}) copy-start(f32[256]{0:T(256)} %param.9) | copy-start | bytes 3076
  0.7 64.6 %copy-start.2 = (f32[1,16]{1,0:T(1,128)S(1)}, f32[1,16]{1,0:T(1,128)}, u32[]{:S(2)}) copy-start(f32[1,16]{1,0:T(1,128)} %param.8) | copy-start | bytes 196
  6.1 4.2 %collective-permute-start = (f32[96,2048]{1,0:T(8,128)S(1)}, f32[96,2048]{1,0:T(8,128)S(1)}, u32[]{:S(2)}, u32[]{:S(2)}) collective-permute-start(f32[96,2048]{1,0:T(8,128)S(1)} %get-tuple-element.8), channel_id=1, source_target_pairs={{0,8},{8,0},{1,9},{9,1},{2,10},{10,2},{3,11},{11,3},{4,12},{12,4},... | collective-permute-start | bytes 2359304 | tf_op jit(solution)/shard_map/ppermute | solution.py:111

commit v3 on v2

--- a/solution.py
+++ b/solution.py
@@ -7,17 +7,20 @@
 
 NJ = 16
 TILE = 128
-NZ, NX, NC, NY = 12, 4, 2, 8
-ROW = ("z", "x", "core")
+NH, NL, NX, NC, NY = 6, 2, 4, 2, 8
+FOLD = 2
+ROW = ("zh", "zl", "x", "core")
 CHUNKS = 4
 AHEAD = 2
 LIMIT = 52 * 2**20
 
 
 def ladder_kernel(core_ref, cols_hbm, left_hbm, tiles_hbm, send_ref, keep_ref,
-                  cols_ref, left_ref, tiles_ref, where_ref, cols_sem, left_sems, tile_sems):
+                  cols_ref, left_ref, tiles_ref, where_ref, acc_ref, cols_sem, left_sems, tile_sems):
     slots, kr = cols_ref.shape
-    half, width = send_ref.shape
+    groups, rows, width = send_ref.shape
+    rows //= FOLD
+    half = groups * rows
     per = kr // CHUNKS
     empty = kr * slots
     stride = NJ + 1
@@ -61,26 +64,31 @@
         first = c * per
         depth = pl.ds(first * TILE, per * TILE)
         left = jnp.concatenate(
-            [left_ref[:, x, side, :, depth] for side in (1 - core, core) for x in range(NX)],
+            [left_ref[:, zl, x, side, :, depth]
+             for side in (1 - core, core) for x in range(NX) for zl in range(NL)],
             axis=0,
         ).reshape(2 * half, per * TILE)
         for j in range(0, NJ, 2):
             span = pl.ds(j * TILE, 2 * TILE)
             right = jnp.concatenate([column(first, j), column(first, j + 1)], axis=1)
             part = jnp.dot(left, right, preferred_element_type=jnp.float32)
-            if c == 0:
-                send_ref[:, span] = part[:half]
-                keep_ref[:, span] = part[half:]
-            else:
-                send_ref[:, span] += part[:half]
-                keep_ref[:, span] += part[half:]
+            if c > 0:
+                part += acc_ref[:, span]
+            if c < CHUNKS - 1:
+                acc_ref[:, span] = part
+                continue
+            at = pl.ds(j * TILE // width * rows, rows)
+            lanes = pl.ds(j * TILE % width, 2 * TILE)
+            for g in range(groups):
+                send_ref[g, at, lanes] = part[g * rows:(g + 1) * rows]
+                keep_ref[g, at, lanes] = part[half + g * rows:half + (g + 1) * rows]
 
 
 def ladder(core, left, integrals, tile_cols):
     kr, slots, _, _ = integrals.shape
     blocks, pairs, depth = left.shape
-    left = left.reshape(NZ, NX, NC, pairs, depth)
-    half = jax.ShapeDtypeStruct((blocks * pairs // NC, NJ * TILE), jnp.float32)
+    left = left.reshape(NH, NL, NX, NC, pairs, depth)
+    half = jax.ShapeDtypeStruct((NX * NL, FOLD * NH * pairs, NJ * TILE // FOLD), jnp.float32)
     return pl.pallas_call(
         ladder_kernel,
         out_shape=(half, half),
@@ -96,6 +104,7 @@
             pltpu.VMEM(left.shape, jnp.bfloat16),
             pltpu.VMEM((kr * slots + 1, TILE, TILE), jnp.bfloat16),
             pltpu.SMEM((kr * (NJ + 1),), jnp.int32),
+            pltpu.VMEM((blocks * pairs, NJ * TILE), jnp.float32),
             pltpu.SemaphoreType.DMA(()),
             pltpu.SemaphoreType.DMA((CHUNKS,)),
             pltpu.SemaphoreType.DMA((CHUNKS,)),
@@ -109,19 +118,18 @@
     core = lax.axis_index("core")
     send, keep = ladder(core, amplitudes, integrals, tile_cols)
     other = lax.ppermute(send, "core", [(0, 1), (1, 0)])
-    chip = (keep + other).reshape(NX, NZ * pairs, NJ * TILE)
-    chip = lax.all_to_all(chip, "x", 0, 0, tiled=True)
-    plane = jnp.sum(chip, axis=0)
-    plane = plane.reshape(NZ, pairs, NY, NJ * TILE // NY).transpose(0, 2, 1, 3)
-    plane = plane.reshape(NZ * NY, pairs, NJ * TILE // NY)
-    owned = lax.all_to_all(plane, ("z", "y"), 0, 0, tiled=True)
-    owned = jnp.sum(owned.reshape(NZ, NY * pairs, NJ * TILE // NY), axis=0, keepdims=True)
+    chip = lax.all_to_all(keep + other, ("x", "zl"), 0, 0, tiled=True)
+    width = NJ * TILE // NY
+    plane = jnp.sum(chip, axis=0).reshape(FOLD, NH, pairs, NY // FOLD, width)
+    plane = plane.transpose(1, 0, 3, 2, 4).reshape(NH * NY, pairs, width)
+    owned = lax.all_to_all(plane, ("zh", "y"), 0, 0, tiled=True)
+    owned = jnp.sum(owned.reshape(NH, NY * pairs, width), axis=0, keepdims=True)
     denom = pair_energy[:, :, None] - col_energy[None, None, :]
     return (owned / denom).astype(jnp.bfloat16)
 
 
 def solution(mesh):
-    fine = Mesh(mesh.devices.reshape(NZ, NX, NC, NY), ("z", "x", "core", "y"))
+    fine = Mesh(mesh.devices.reshape(NH, NL, NX, NC, NY), ("zh", "zl", "x", "core", "y"))
     in_specs = (
         P(None, "y", ROW),
         P(ROW, None, None, None),

time: 66.2 us -> 64.2 us (0.970)
  blocking collectives: 54.4 us -> 52.6 us
    all_to_all x2, blocking collectives: 54.4 us -> 52.6 us  [the longest x1 33.5 us: per_device(): owned = lax.all_to_all(plane, ('zh', 'y'), 0, 0, tiled=True)]
where the time goes in v3:
time: 64.2 us; the launch traced here: 64 us
  blocking collectives  52.6 us (82%)
  Pallas kernels  5.39 us (8%)
  waiting for transfers between devices  2.25 us (4%)
  starting transfers between devices  1.92 us (3%)
  local copies, waits for them, and re-layouts  0.89 us (1%)
  other arithmetic  0.84 us (1%)
    all_to_all x1, blocking collectives, per_device(): owned = lax.all_to_all(plane, ('zh', 'y'), 0, 0, tiled=True)  33.5 us
    all_to_all x1, blocking collectives, per_device(): chip = lax.all_to_all(keep + other, ('x', 'zl'), 0, 0, tiled=True)  19.1 us
    pallas_call x1, Pallas kernels, ladder(): pl.pallas_call(ladder_kernel, out_shape=(half, half), in_specs=[pl.BlockS...  5.39 us
    ppermute x1, waiting for transfers between devices, per_device(): other = lax.ppermute(send, 'core', [(0, 1), (1, 0)])  2.25 us
    ppermute x1, starting transfers between devices, per_device(): other = lax.ppermute(send, 'core', [(0, 1), (1, 0)])  1.92 us
  transfers between devices with their start and end apart: 1, of which 1 were waited for; matrix products, arithmetic and copies ran while one was open for 0% of the time, Pallas kernels for 0%

profile of v3, /device:TPU:8, one launch (start us, length us, event | category | flops | bytes accessed | tf_op | source)
XLA Modules:
  0.0 64.0 jit_solution(5219985881395090835)
XLA Ops:
  0.0 0.0 copy-start.1
  0.0 0.0 copy-start.2
  0.0 0.0 copy-start
  0.0 0.7 %copy-done = s32[32,8]{0,1:T(8,128)S(1)} copy-done((s32[32,8]{0,1:T(8,128)S(1)}, s32[32,8]{0,1:T(8,128)}, u32[]{:S(2)}) %copy-start) | copy-done | bytes 1048
  0.7 5.4 %shard_map.58 = (f32[8,24,1024]{2,1,0:T(8,128)S(1)}, f32[8,24,1024]{2,1,0:T(8,128)S(1)}) custom-call(s32[1]{0:T(128)} %bitcast.core_ref, s32[8,32]{1,0:T(8,128)S(1)} %bitcast.11, bf16[6,2,4,2,2,4096]{5,4,3,2,1,0:T(2,128)(2,1)} %bitcast.13, bf16[256,128,128]{2,1,0:T(8,128)(2,1)} %bitcast.12), custom_call_target="tpu_custom_call" | custom-call | tf_op jit(solution)/shard_map/pallas_call | solution.py:92
  6.1 1.9 %collective-permute-start = (f32[8,24,1024]{2,1,0:T(8,128)S(1)}, f32[8,24,1024]{2,1,0:T(8,128)S(1)}, u32[]{:S(2)}, u32[]{:S(2)}) collective-permute-start(f32[8,24,1024]{2,1,0:T(8,128)S(1)} %get-tuple-element.8), channel_id=1, source_target_pairs={{0,8},{8,0},{1,9},{9,1},{2,10},{10,2},{3,11},{11,3},{4,12},{12,4},... | collective-permute-start | bytes 2359304 | tf_op jit(solution)/shard_map/ppermute | solution.py:120
  8.0 2.3 %collective-permute-done = f32[8,24,1024]{2,1,0:T(8,128)S(1)} collective-permute-done((f32[8,24,1024]{2,1,0:T(8,128)S(1)}, f32[8,24,1024]{2,1,0:T(8,128)S(1)}, u32[]{:S(2)}, u32[]{:S(2)}) %collective-permute-start) | collective-permute-done | bytes 786464 | tf_op jit(solution)/shard_map/ppermute | solution.py:120
  10.3 0.1 add.3
  10.4 19.1 %all_to_all.10 = f32[8,24,1024]{2,1,0:T(8,128)S(1)} all-to-all(f32[8,24,1024]{2,1,0:T(8,128)S(1)} %add.3), channel_id=1, replica_groups=mesh['zh'=6,'zl'=2,'x'=4,'core'=2,'y'=8] {'x','zl'}, dimensions={0} | all-to-all | bytes 1572864 | tf_op jit(solution)/shard_map/all_to_all | solution.py:121
  29.6 0.1 copy.6
  29.7 33.5 %all_to_all.11 = f32[48,2,256]{2,1,0:T(2,128)S(1)} all-to-all(f32[48,2,256]{2,1,0:T(2,128)S(1)} %bitcast.15), channel_id=1, replica_groups=mesh['zh'=6,'zl'=2,'x'=4,'core'=2,'y'=8] {'zh','y'}, dimensions={0} | all-to-all | bytes 196608 | tf_op jit(solution)/shard_map/all_to_all | solution.py:125
  63.2 0.1 reshape.90
  63.3 0.0 copy-done.1
  63.3 0.0 copy-done.2
  63.3 0.7 %fusion = bf16[1,16,256]{2,1,0:T(8,128)(2,1)} fusion(f32[16,256]{1,0:T(8,128)S(1)} %reduce_sum.21, f32[256]{0:T(256)S(1)} %copy-done.1, f32[16]{0:T(128)S(1)} %bitcast.16), kind=kLoop, calls=%fused_computation.1 | loop fusion | flops 12288 | bytes 25664 | tf_op jit(solution)/shard_map/convert_element_type | solution.py:128
  (3 shorter events, 0.1 us)
Async XLA Ops:
  0.0 63.3 %copy-start.1 = (f32[256]{0:T(256)S(1)}, f32[256]{0:T(256)}, u32[]{:S(2)}) copy-start(f32[256]{0:T(256)} %param.9) | copy-start | bytes 3076
  0.0 63.3 %copy-start.2 = (f32[1,16]{1,0:T(1,128)S(1)}, f32[1,16]{1,0:T(1,128)}, u32[]{:S(2)}) copy-start(f32[1,16]{1,0:T(1,128)} %param.8) | copy-start | bytes 196
  0.0 0.7 %copy-start = (s32[32,8]{0,1:T(8,128)S(1)}, s32[32,8]{0,1:T(8,128)}, u32[]{:S(2)}) copy-start(s32[32,8]{0,1:T(8,128)} %param.7) | copy-start | bytes 3076
  6.1 4.2 %collective-permute-start = (f32[8,24,1024]{2,1,0:T(8,128)S(1)}, f32[8,24,1024]{2,1,0:T(8,128)S(1)}, u32[]{:S(2)}, u32[]{:S(2)}) collective-permute-start(f32[8,24,1024]{2,1,0:T(8,128)S(1)} %get-tuple-element.8), channel_id=1, source_target_pairs={{0,8},{8,0},{1,9},{9,1},{2,10},{10,2},{3,11},{11,3},{4,12},{12,4},... | collective-permute-start | bytes 2359304 | tf_op jit(solution)/shard_map/ppermute | solution.py:120

commit v4 on v3

--- a/solution.py
+++ b/solution.py
@@ -10,9 +10,10 @@
 NH, NL, NX, NC, NY = 6, 2, 4, 2, 8
 FOLD = 2
 ROW = ("zh", "zl", "x", "core")
-CHUNKS = 4
-AHEAD = 2
-LIMIT = 52 * 2**20
+BOUNDS = (0, 4, 8, 14, 20, 26, 32)
+CHUNKS = len(BOUNDS) - 1
+AHEAD = 3
+LIMIT = 32 * 2**20
 
 
 def ladder_kernel(core_ref, cols_hbm, left_hbm, tiles_hbm, send_ref, keep_ref,
@@ -21,14 +22,14 @@
     groups, rows, width = send_ref.shape
     rows //= FOLD
     half = groups * rows
-    per = kr // CHUNKS
     empty = kr * slots
     stride = NJ + 1
     core = core_ref[0]
 
     def copies(c):
-        depth = pl.ds(c * per * TILE, per * TILE)
-        span = pl.ds(c * per * slots, per * slots)
+        first, per = BOUNDS[c], BOUNDS[c + 1] - BOUNDS[c]
+        depth = pl.ds(first * TILE, per * TILE)
+        span = pl.ds(first * slots, per * slots)
         return (
             pltpu.make_async_copy(left_hbm.at[..., depth], left_ref.at[..., depth], left_sems.at[c]),
             pltpu.make_async_copy(tiles_hbm.at[span], tiles_ref.at[span], tile_sems.at[c]),
@@ -51,7 +52,7 @@
         for s in range(slots):
             where_ref[k * stride + found[s] + 1] = k * slots + s
 
-    def column(first, j):
+    def column(first, per, j):
         return jnp.concatenate(
             [tiles_ref[where_ref[(first + i) * stride + j + 1]] for i in range(per)], axis=0
         )
@@ -61,7 +62,7 @@
             copy.wait()
         if c + AHEAD < CHUNKS:
             start(c + AHEAD)
-        first = c * per
+        first, per = BOUNDS[c], BOUNDS[c + 1] - BOUNDS[c]
         depth = pl.ds(first * TILE, per * TILE)
         left = jnp.concatenate(
             [left_ref[:, zl, x, side, :, depth]
@@ -70,7 +71,7 @@
         ).reshape(2 * half, per * TILE)
         for j in range(0, NJ, 2):
             span = pl.ds(j * TILE, 2 * TILE)
-            right = jnp.concatenate([column(first, j), column(first, j + 1)], axis=1)
+            right = jnp.concatenate([column(first, per, j), column(first, per, j + 1)], axis=1)
             part = jnp.dot(left, right, preferred_element_type=jnp.float32)
             if c > 0:
                 part += acc_ref[:, span]
@@ -110,7 +111,12 @@
             pltpu.SemaphoreType.DMA((CHUNKS,)),
         ],
         compiler_params=pltpu.CompilerParams(vmem_limit_bytes=LIMIT),
-    )(core.reshape(1), tile_cols.T, left, integrals.reshape(kr * slots, TILE, TILE))
+    )(
+        core.reshape(1),
+        pltpu.with_memory_space_constraint(tile_cols.T, pltpu.HBM),
+        pltpu.with_memory_space_constraint(left, pltpu.HBM),
+        pltpu.with_memory_space_constraint(integrals.reshape(kr * slots, TILE, TILE), pltpu.HBM),
+    )
 
 
 def per_device(amplitudes, integrals, tile_cols, pair_energy, col_energy):

time: 64.2 us -> 63.3 us (0.986)
  local copies, waits for them, and re-layouts: 0.89 us -> 0.18 us
    unnamed x6 -> x4, local copies, waits for them, and re-layouts: 0.72 us -> 0.01 us
where the time goes in v4:
time: 63.3 us; the launch traced here: 63.1 us
  blocking collectives  52.6 us (83%)
  Pallas kernels  5.25 us (8%)
  waiting for transfers between devices  2.25 us (4%)
  starting transfers between devices  1.92 us (3%)
  other arithmetic  0.84 us (1%)
    all_to_all x1, blocking collectives, per_device(): owned = lax.all_to_all(plane, ('zh', 'y'), 0, 0, tiled=True)  33.5 us
    all_to_all x1, blocking collectives, per_device(): chip = lax.all_to_all(keep + other, ('x', 'zl'), 0, 0, tiled=True)  19.1 us
    pallas_call x1, Pallas kernels, ladder(): pl.pallas_call(ladder_kernel, out_shape=(half, half), in_specs=[pl.BlockS...  5.25 us
    ppermute x1, waiting for transfers between devices, per_device(): other = lax.ppermute(send, 'core', [(0, 1), (1, 0)])  2.25 us
    ppermute x1, starting transfers between devices, per_device(): other = lax.ppermute(send, 'core', [(0, 1), (1, 0)])  1.92 us
  transfers between devices with their start and end apart: 1, of which 1 were waited for; matrix products, arithmetic and copies ran while one was open for 0% of the time, Pallas kernels for 0%

profile of v4, /device:TPU:8, one launch (start us, length us, event | category | flops | bytes accessed | tf_op | source)
XLA Modules:
  0.0 63.1 jit_solution(12402097755567796290)
XLA Ops:
  0.0 0.0 copy-start
  0.0 0.0 copy-start.1
  0.0 5.2 %shard_map.58 = (f32[8,24,1024]{2,1,0:T(8,128)S(1)}, f32[8,24,1024]{2,1,0:T(8,128)S(1)}) custom-call(s32[1]{0:T(128)} %bitcast.core_ref, s32[8,32]{1,0:T(8,128)} %bitcast.15, bf16[6,2,4,2,2,4096]{5,4,3,2,1,0:T(2,128)(2,1)} %bitcast.12, bf16[256,128,128]{2,1,0:T(8,128)(2,1)} %bitcast.11), custom_call_target="tpu_custom_call" | custom-call | tf_op jit(solution)/shard_map/pallas_call | solution.py:93
  5.3 1.9 %collective-permute-start = (f32[8,24,1024]{2,1,0:T(8,128)S(1)}, f32[8,24,1024]{2,1,0:T(8,128)S(1)}, u32[]{:S(2)}, u32[]{:S(2)}) collective-permute-start(f32[8,24,1024]{2,1,0:T(8,128)S(1)} %get-tuple-element.8), channel_id=1, source_target_pairs={{0,8},{8,0},{1,9},{9,1},{2,10},{10,2},{3,11},{11,3},{4,12},{12,4},... | collective-permute-start | bytes 2359304 | tf_op jit(solution)/shard_map/ppermute | solution.py:126
  7.2 2.3 %collective-permute-done = f32[8,24,1024]{2,1,0:T(8,128)S(1)} collective-permute-done((f32[8,24,1024]{2,1,0:T(8,128)S(1)}, f32[8,24,1024]{2,1,0:T(8,128)S(1)}, u32[]{:S(2)}, u32[]{:S(2)}) %collective-permute-start) | collective-permute-done | bytes 786464 | tf_op jit(solution)/shard_map/ppermute | solution.py:126
  9.4 0.1 add.3
  9.6 19.1 %all_to_all.10 = f32[8,24,1024]{2,1,0:T(8,128)S(1)} all-to-all(f32[8,24,1024]{2,1,0:T(8,128)S(1)} %add.3), channel_id=1, replica_groups=mesh['zh'=6,'zl'=2,'x'=4,'core'=2,'y'=8] {'x','zl'}, dimensions={0} | all-to-all | bytes 1572864 | tf_op jit(solution)/shard_map/all_to_all | solution.py:127
  28.8 0.1 copy.6
  28.8 33.5 %all_to_all.11 = f32[48,2,256]{2,1,0:T(2,128)S(1)} all-to-all(f32[48,2,256]{2,1,0:T(2,128)S(1)} %bitcast.14), channel_id=1, replica_groups=mesh['zh'=6,'zl'=2,'x'=4,'core'=2,'y'=8] {'zh','y'}, dimensions={0} | all-to-all | bytes 196608 | tf_op jit(solution)/shard_map/all_to_all | solution.py:131
  62.3 0.1 reshape.90
  62.4 0.0 copy-done
  62.4 0.0 copy-done.1
  62.4 0.7 %fusion = bf16[1,16,256]{2,1,0:T(8,128)(2,1)} fusion(f32[16,256]{1,0:T(8,128)S(1)} %reduce_sum.21, f32[256]{0:T(256)S(1)} %copy-done, f32[16]{0:T(128)S(1)} %bitcast.16), kind=kLoop, calls=%fused_computation.1 | loop fusion | flops 12288 | bytes 25664 | tf_op jit(solution)/shard_map/convert_element_type | solution.py:134
  (3 shorter events, 0.1 us)
Async XLA Ops:
  0.0 62.4 %copy-start = (f32[256]{0:T(256)S(1)}, f32[256]{0:T(256)}, u32[]{:S(2)}) copy-start(f32[256]{0:T(256)} %param.9) | copy-start | bytes 3076
  0.0 62.4 %copy-start.1 = (f32[1,16]{1,0:T(1,128)S(1)}, f32[1,16]{1,0:T(1,128)}, u32[]{:S(2)}) copy-start(f32[1,16]{1,0:T(1,128)} %param.8) | copy-start | bytes 196
  5.3 4.2 %collective-permute-start = (f32[8,24,1024]{2,1,0:T(8,128)S(1)}, f32[8,24,1024]{2,1,0:T(8,128)S(1)}, u32[]{:S(2)}, u32[]{:S(2)}) collective-permute-start(f32[8,24,1024]{2,1,0:T(8,128)S(1)} %get-tuple-element.8), channel_id=1, source_target_pairs={{0,8},{8,0},{1,9},{9,1},{2,10},{10,2},{3,11},{11,3},{4,12},{12,4},... | collective-permute-start | bytes 2359304 | tf_op jit(solution)/shard_map/ppermute | solution.py:126

commit v5 on v4

--- a/solution.py
+++ b/solution.py
@@ -9,6 +9,12 @@
 TILE = 128
 NH, NL, NX, NC, NY = 6, 2, 4, 2, 8
 FOLD = 2
+Z_ORDER = tuple((i + NH // 2) % NH for i in range(NH))
+Y_ORDER = tuple((i + NY // 2) % NY for i in range(NY))
+X_ORDER = (2, 3, 0, 1)
+L_ORDER = (1, 0)
+PLANE = [x * NL + zl for x in X_ORDER for zl in L_ORDER]
+COLUMN = [zh * NY + y for zh in Z_ORDER for y in Y_ORDER]
 ROW = ("zh", "zl", "x", "core")
 BOUNDS = (0, 4, 8, 14, 20, 26, 32)
 CHUNKS = len(BOUNDS) - 1
@@ -65,8 +71,9 @@
         first, per = BOUNDS[c], BOUNDS[c + 1] - BOUNDS[c]
         depth = pl.ds(first * TILE, per * TILE)
         left = jnp.concatenate(
-            [left_ref[:, zl, x, side, :, depth]
-             for side in (1 - core, core) for x in range(NX) for zl in range(NL)],
+            [left_ref[pl.ds(zh, NH // 2), zl, x, side, :, depth]
+             for side in (1 - core, core) for x in X_ORDER for zl in L_ORDER
+             for zh in (NH // 2, 0)],
             axis=0,
         ).reshape(2 * half, per * TILE)
         for j in range(0, NJ, 2):
@@ -78,7 +85,7 @@
             if c < CHUNKS - 1:
                 acc_ref[:, span] = part
                 continue
-            at = pl.ds(j * TILE // width * rows, rows)
+            at = pl.ds((1 - j * TILE // width) * rows, rows)
             lanes = pl.ds(j * TILE % width, 2 * TILE)
             for g in range(groups):
                 send_ref[g, at, lanes] = part[g * rows:(g + 1) * rows]
@@ -124,12 +131,13 @@
     core = lax.axis_index("core")
     send, keep = ladder(core, amplitudes, integrals, tile_cols)
     other = lax.ppermute(send, "core", [(0, 1), (1, 0)])
-    chip = lax.all_to_all(keep + other, ("x", "zl"), 0, 0, tiled=True)
+    chip = lax.all_to_all(keep + other, ("x", "zl"), 0, 0, tiled=True, axis_index_groups=[PLANE])
     width = NJ * TILE // NY
     plane = jnp.sum(chip, axis=0).reshape(FOLD, NH, pairs, NY // FOLD, width)
     plane = plane.transpose(1, 0, 3, 2, 4).reshape(NH * NY, pairs, width)
-    owned = lax.all_to_all(plane, ("zh", "y"), 0, 0, tiled=True)
+    owned = lax.all_to_all(plane, ("zh", "y"), 0, 0, tiled=True, axis_index_groups=[COLUMN])
     owned = jnp.sum(owned.reshape(NH, NY * pairs, width), axis=0, keepdims=True)
+    owned = jnp.roll(owned, NY // 2 * pairs, axis=1)
     denom = pair_energy[:, :, None] - col_energy[None, None, :]
     return (owned / denom).astype(jnp.bfloat16)
 

time: 63.3 us -> 55.6 us (0.88)
  blocking collectives: 52.6 us -> 44.9 us
    all_to_all x2, blocking collectives: 52.6 us -> 44.9 us  [the longest x1 27.7 us: per_device(): lax.all_to_all(plane, ('zh', 'y'), 0, 0, tiled=True, axis_index_groups=[C...]
where the time goes in v5:
time: 55.6 us; the launch traced here: 55.4 us
  blocking collectives  44.9 us (81%)
  Pallas kernels  5.25 us (9%)
  waiting for transfers between devices  2.25 us (4%)
  starting transfers between devices  1.92 us (3%)
  other arithmetic  0.84 us (2%)
    all_to_all x1, blocking collectives, per_device(): lax.all_to_all(plane, ('zh', 'y'), 0, 0, tiled=True, axis_index_groups=[C...  27.7 us
    all_to_all x1, blocking collectives, per_device(): lax.all_to_all(keep + other, ('x', 'zl'), 0, 0, tiled=True, axis_index_gr...  17.2 us
    pallas_call x1, Pallas kernels, ladder(): pl.pallas_call(ladder_kernel, out_shape=(half, half), in_specs=[pl.BlockS...  5.25 us
    ppermute x1, waiting for transfers between devices, per_device(): other = lax.ppermute(send, 'core', [(0, 1), (1, 0)])  2.25 us
    ppermute x1, starting transfers between devices, per_device(): other = lax.ppermute(send, 'core', [(0, 1), (1, 0)])  1.92 us
  transfers between devices with their start and end apart: 1, of which 1 were waited for; matrix products, arithmetic and copies ran while one was open for 0% of the time, Pallas kernels for 0%

profile of v5, /device:TPU:8, one launch (start us, length us, event | category | flops | bytes accessed | tf_op | source)
XLA Modules:
  0.0 55.4 jit_solution(7947712053182693153)
XLA Ops:
  0.0 0.0 copy-start
  0.0 0.0 copy-start.1
  0.0 5.2 %shard_map.58 = (f32[8,24,1024]{2,1,0:T(8,128)S(1)}, f32[8,24,1024]{2,1,0:T(8,128)S(1)}) custom-call(s32[1]{0:T(128)} %bitcast.core_ref, s32[8,32]{1,0:T(8,128)} %bitcast.13, bf16[6,2,4,2,2,4096]{5,4,3,2,1,0:T(2,128)(2,1)} %bitcast.9, bf16[256,128,128]{2,1,0:T(8,128)(2,1)} %bitcast.8), custom_call_target="tpu_custom_call" | custom-call | tf_op jit(solution)/shard_map/pallas_call | solution.py:100
  5.3 1.9 %collective-permute-start = (f32[8,24,1024]{2,1,0:T(8,128)S(1)}, f32[8,24,1024]{2,1,0:T(8,128)S(1)}, u32[]{:S(2)}, u32[]{:S(2)}) collective-permute-start(f32[8,24,1024]{2,1,0:T(8,128)S(1)} %get-tuple-element.8), channel_id=1, source_target_pairs={{0,8},{8,0},{1,9},{9,1},{2,10},{10,2},{3,11},{11,3},{4,12},{12,4},... | collective-permute-start | bytes 2359304 | tf_op jit(solution)/shard_map/ppermute | solution.py:133
  7.2 2.3 %collective-permute-done = f32[8,24,1024]{2,1,0:T(8,128)S(1)} collective-permute-done((f32[8,24,1024]{2,1,0:T(8,128)S(1)}, f32[8,24,1024]{2,1,0:T(8,128)S(1)}, u32[]{:S(2)}, u32[]{:S(2)}) %collective-permute-start) | collective-permute-done | bytes 786464 | tf_op jit(solution)/shard_map/ppermute | solution.py:133
  9.4 0.1 add.3
  9.6 17.2 %all_to_all.10 = f32[8,24,1024]{2,1,0:T(8,128)S(1)} all-to-all(f32[8,24,1024]{2,1,0:T(8,128)S(1)} %add.3), channel_id=1, replica_groups={{96,32,112,48,64,0,80,16},{97,33,113,49,65,1,81,17},{98,34,114,50,66,2,..., dimensions={0} | all-to-all | bytes 1572864 | tf_op jit(solution)/shard_map/all_to_all | solution.py:134
  26.8 0.1 copy.6
  26.9 27.7 %all_to_all.11 = f32[48,2,256]{2,1,0:T(2,128)S(1)} all-to-all(f32[48,2,256]{2,1,0:T(2,128)S(1)} %bitcast.11), channel_id=1, replica_groups={{388,389,390,391,384,385,386,387,516,517,518,519,512,513,514,515,644,64..., dimensions={0} | all-to-all | bytes 196608 | tf_op jit(solution)/shard_map/all_to_all | solution.py:138
  54.6 0.1 reshape.110
  54.7 0.0 copy-done
  54.7 0.0 copy-done.1
  54.8 0.7 %fusion = bf16[1,16,256]{2,1,0:T(8,128)(2,1)} fusion(f32[1,8,256]{2,1,0:T(8,128)S(1)} %get-tuple-element.10, f32[1,8,256]{2,1,0:T(8,128)S(1)} %get-tuple-element.9, f32[256]{0:T(256)S(1)} %copy-done, f32[16]{0:T(128)S(1)} %bitcast.14), kind=kLoop, calls=%fused_computation.1 | loop fusion | flops 16384 | bytes 25664 | tf_op jit(solution)/shard_map/convert_element_type | solution.py:142
  (4 shorter events, 0.1 us)
Async XLA Ops:
  0.0 54.7 %copy-start = (f32[256]{0:T(256)S(1)}, f32[256]{0:T(256)}, u32[]{:S(2)}) copy-start(f32[256]{0:T(256)} %param.9) | copy-start | bytes 3076
  0.0 54.7 %copy-start.1 = (f32[1,16]{1,0:T(1,128)S(1)}, f32[1,16]{1,0:T(1,128)}, u32[]{:S(2)}) copy-start(f32[1,16]{1,0:T(1,128)} %param.8) | copy-start | bytes 196
  5.3 4.2 %collective-permute-start = (f32[8,24,1024]{2,1,0:T(8,128)S(1)}, f32[8,24,1024]{2,1,0:T(8,128)S(1)}, u32[]{:S(2)}, u32[]{:S(2)}) collective-permute-start(f32[8,24,1024]{2,1,0:T(8,128)S(1)} %get-tuple-element.8), channel_id=1, source_target_pairs={{0,8},{8,0},{1,9},{9,1},{2,10},{10,2},{3,11},{11,3},{4,12},{12,4},... | collective-permute-start | bytes 2359304 | tf_op jit(solution)/shard_map/ppermute | solution.py:133

commit v6 on v5

--- a/solution.py
+++ b/solution.py
@@ -9,7 +9,7 @@
 TILE = 128
 NH, NL, NX, NC, NY = 6, 2, 4, 2, 8
 FOLD = 2
-Z_ORDER = tuple((i + NH // 2) % NH for i in range(NH))
+Z_ORDER = tuple((i + 4) % NH for i in range(NH))
 Y_ORDER = tuple((i + NY // 2) % NY for i in range(NY))
 X_ORDER = (2, 3, 0, 1)
 L_ORDER = (1, 0)
@@ -71,9 +71,9 @@
         first, per = BOUNDS[c], BOUNDS[c + 1] - BOUNDS[c]
         depth = pl.ds(first * TILE, per * TILE)
         left = jnp.concatenate(
-            [left_ref[pl.ds(zh, NH // 2), zl, x, side, :, depth]
+            [left_ref[zh, zl, x, side, :, depth]
              for side in (1 - core, core) for x in X_ORDER for zl in L_ORDER
-             for zh in (NH // 2, 0)],
+             for zh in (pl.ds(4, NH - 4), pl.ds(0, 4))],
             axis=0,
         ).reshape(2 * half, per * TILE)
         for j in range(0, NJ, 2):

time: 55.6 us -> 55.2 us (level)
  the two profiles are of different devices: /device:TPU:8 before, /device:TPU:4 now
where the time goes in v6:
time: 55.2 us; the launch traced here: 55 us
  blocking collectives  44.5 us (81%)
  Pallas kernels  5.25 us (10%)
  waiting for transfers between devices  2.25 us (4%)
  starting transfers between devices  1.92 us (3%)
  other arithmetic  0.84 us (2%)
    all_to_all x1, blocking collectives, per_device(): lax.all_to_all(keep + other, ('x', 'zl'), 0, 0, tiled=True, axis_index_gr...  24.1 us
    all_to_all x1, blocking collectives, per_device(): lax.all_to_all(plane, ('zh', 'y'), 0, 0, tiled=True, axis_index_groups=[C...  20.4 us
    pallas_call x1, Pallas kernels, ladder(): pl.pallas_call(ladder_kernel, out_shape=(half, half), in_specs=[pl.BlockS...  5.25 us
    ppermute x1, waiting for transfers between devices, per_device(): other = lax.ppermute(send, 'core', [(0, 1), (1, 0)])  2.25 us
    ppermute x1, starting transfers between devices, per_device(): other = lax.ppermute(send, 'core', [(0, 1), (1, 0)])  1.92 us
  transfers between devices with their start and end apart: 1, of which 1 were waited for; matrix products, arithmetic and copies ran while one was open for 0% of the time, Pallas kernels for 0%

profile of v6, /device:TPU:4, one launch (start us, length us, event | category | flops | bytes accessed | tf_op | source)
XLA Modules:
  0.0 55.0 jit_solution(10710149748664147722)
XLA Ops:
  0.0 0.0 copy-start
  0.0 0.0 copy-start.1
  0.0 5.3 %shard_map.58 = (f32[8,24,1024]{2,1,0:T(8,128)S(1)}, f32[8,24,1024]{2,1,0:T(8,128)S(1)}) custom-call(s32[1]{0:T(128)} %bitcast.core_ref, s32[8,32]{1,0:T(8,128)} %bitcast.13, bf16[6,2,4,2,2,4096]{5,4,3,2,1,0:T(2,128)(2,1)} %bitcast.9, bf16[256,128,128]{2,1,0:T(8,128)(2,1)} %bitcast.8), custom_call_target="tpu_custom_call" | custom-call | tf_op jit(solution)/shard_map/pallas_call | solution.py:100
  5.3 1.9 %collective-permute-start = (f32[8,24,1024]{2,1,0:T(8,128)S(1)}, f32[8,24,1024]{2,1,0:T(8,128)S(1)}, u32[]{:S(2)}, u32[]{:S(2)}) collective-permute-start(f32[8,24,1024]{2,1,0:T(8,128)S(1)} %get-tuple-element.8), channel_id=1, source_target_pairs={{0,8},{8,0},{1,9},{9,1},{2,10},{10,2},{3,11},{11,3},{4,12},{12,4},... | collective-permute-start | bytes 2359304 | tf_op jit(solution)/shard_map/ppermute | solution.py:133
  7.2 2.3 %collective-permute-done = f32[8,24,1024]{2,1,0:T(8,128)S(1)} collective-permute-done((f32[8,24,1024]{2,1,0:T(8,128)S(1)}, f32[8,24,1024]{2,1,0:T(8,128)S(1)}, u32[]{:S(2)}, u32[]{:S(2)}) %collective-permute-start) | collective-permute-done | bytes 786464 | tf_op jit(solution)/shard_map/ppermute | solution.py:133
  9.4 0.1 add.3
  9.6 24.1 %all_to_all.10 = f32[8,24,1024]{2,1,0:T(8,128)S(1)} all-to-all(f32[8,24,1024]{2,1,0:T(8,128)S(1)} %add.3), channel_id=1, replica_groups={{96,32,112,48,64,0,80,16},{97,33,113,49,65,1,81,17},{98,34,114,50,66,2,..., dimensions={0} | all-to-all | bytes 1572864 | tf_op jit(solution)/shard_map/all_to_all | solution.py:134
  33.7 0.1 copy.6
  33.8 20.4 %all_to_all.11 = f32[48,2,256]{2,1,0:T(2,128)S(1)} all-to-all(f32[48,2,256]{2,1,0:T(2,128)S(1)} %bitcast.11), channel_id=1, replica_groups={{516,517,518,519,512,513,514,515,644,645,646,647,640,641,642,643,4,5,6,..., dimensions={0} | all-to-all | bytes 196608 | tf_op jit(solution)/shard_map/all_to_all | solution.py:138
  54.2 0.1 reshape.110
  54.3 0.0 copy-done
  54.3 0.0 copy-done.1
  54.3 0.7 %fusion = bf16[1,16,256]{2,1,0:T(8,128)(2,1)} fusion(f32[1,8,256]{2,1,0:T(8,128)S(1)} %get-tuple-element.10, f32[1,8,256]{2,1,0:T(8,128)S(1)} %get-tuple-element.9, f32[256]{0:T(256)S(1)} %copy-done, f32[16]{0:T(128)S(1)} %bitcast.14), kind=kLoop, calls=%fused_computation.1 | loop fusion | flops 16384 | bytes 25664 | tf_op jit(solution)/shard_map/convert_element_type | solution.py:142
  (4 shorter events, 0.1 us)
Async XLA Ops:
  0.0 54.3 %copy-start = (f32[256]{0:T(256)S(1)}, f32[256]{0:T(256)}, u32[]{:S(2)}) copy-start(f32[256]{0:T(256)} %param.9) | copy-start | bytes 3076
  0.0 54.3 %copy-start.1 = (f32[1,16]{1,0:T(1,128)S(1)}, f32[1,16]{1,0:T(1,128)}, u32[]{:S(2)}) copy-start(f32[1,16]{1,0:T(1,128)} %param.8) | copy-start | bytes 196
  5.3 4.2 %collective-permute-start = (f32[8,24,1024]{2,1,0:T(8,128)S(1)}, f32[8,24,1024]{2,1,0:T(8,128)S(1)}, u32[]{:S(2)}, u32[]{:S(2)}) collective-permute-start(f32[8,24,1024]{2,1,0:T(8,128)S(1)} %get-tuple-element.8), channel_id=1, source_target_pairs={{0,8},{8,0},{1,9},{9,1},{2,10},{10,2},{3,11},{11,3},{4,12},{12,4},... | collective-permute-start | bytes 2359304 | tf_op jit(solution)/shard_map/ppermute | solution.py:133
